TPU v7x, 32 devices: a whole 2x2x4 slice. The times are simulated.
32 devices in a mesh: dp: 8 (over y, x, core), ctx: 4 (over z).
Axes of the slice: x: 2, y: 2, z: 4, core: 2. Of those that a mesh axis runs over, the one named last changes fastest.
Arguments:
- output_gradient: float32 [8, 8, 32768], P('dp', None, 'ctx'), may hold values from -6 to 6
- input_spectrum: float32 [8, 8, 2, 32768], P('dp', None, None, 'ctx'), may hold values from -0.0390625 to 0.0390625
- filter_spectrum: float32 [8, 2, 32768], P(None, None, 'ctx'), may hold values from -12 to 12
Outputs:
- input_gradient: float32 [8, 8, 32768], P('dp', None, 'ctx')
- filter_gradient: float32 [8, 2, 32768], P(None, None, ('ctx', 'dp'))
All inputs are finite; a program needn't handle non-finite values.
Results may differ from a plain program's by a relative error of at most 0.0001.
Values sent between devices are 32-bit elements; how exact they have to be, the bound alone decides.
A program may use at most 128 MiB of HBM per device.

v0:
```python
import math

import jax
import jax.numpy as jnp
from jax import lax
from jax.sharding import PartitionSpec as P

precise = lax.Precision.HIGHEST


def partner_2(value, axis, apart):
    mask = 2**apart
    pairs = [(source, source ^ mask) for source in range(lax.axis_size(axis))]
    return lax.ppermute(value, axis, pairs)


def rotate(real_part, imag_part, phase):
    cosine = jnp.cos(phase)
    sine = jnp.sin(phase)
    return (real_part * cosine - imag_part * sine, real_part * sine + imag_part * cosine)


def reverse(index, sections):
    result = jnp.zeros_like(index)
    for level in range(sections):
        result = result | (index >> level & 1) << sections - 1 - level
    return result


def square_table(order_size, sign_value):
    series = jnp.arange(order_size, dtype=jnp.int32)
    powers = series[:, None] * series[None, :] % order_size
    phase = sign_value * 2.0 * math.pi / order_size * powers.astype(jnp.float32)
    return (jnp.cos(phase), jnp.sin(phase))


def complex_product(form, left_real, left_imag, right_real, right_imag):
    real_out = jnp.einsum(form, left_real, right_real, precision=precise) - jnp.einsum(
        form, left_imag, right_imag, precision=precise
    )
    imag_out = jnp.einsum(form, left_real, right_imag, precision=precise) + jnp.einsum(
        form, left_imag, right_real, precision=precise
    )
    return (real_out, imag_out)


def local_dft(real_part, imag_part, sign_value):
    full_shape = real_part.shape
    length = full_shape[-1]
    inner_size = 1 << (length.bit_length() - 1) // 2
    outer_size = length // inner_size
    real_part = real_part.reshape(-1, outer_size, inner_size)
    imag_part = imag_part.reshape(-1, outer_size, inner_size)
    cos_outer, sin_outer = square_table(outer_size, sign_value)
    first_real, first_imag = complex_product(
        "nk,ska->sna", cos_outer, sin_outer, real_part, imag_part
    )
    series_outer = jnp.arange(outer_size, dtype=jnp.int32)
    series_inner = jnp.arange(inner_size, dtype=jnp.int32)
    powers = series_outer[:, None] * series_inner[None, :]
    first_real, first_imag = rotate(
        first_real, first_imag, sign_value * 2.0 * math.pi / length * powers.astype(jnp.float32)
    )
    cos_inner, sin_inner = square_table(inner_size, sign_value)
    last_real, last_imag = complex_product(
        "ma,sna->smn", cos_inner, sin_inner, first_real, first_imag
    )
    return (last_real.reshape(full_shape), last_imag.reshape(full_shape))


def signals(samples, positions, length):
    phase = -0.5 * math.pi / length * positions.astype(jnp.float32)
    return jnp.stack([samples * jnp.cos(phase), samples * jnp.sin(phase)], axis=2)


def descend(own_field, far_field, self_index, level_bit):
    half_span = 1 << level_bit
    full_span = 2 * half_span
    within = self_index % full_span
    upper_half = within >= half_span
    phase = -2.0 * math.pi / full_span * (within - half_span).astype(jnp.float32)
    summed = own_field + far_field
    differ = far_field - own_field
    turned_real, turned_imag = rotate(differ[:, :, 0], differ[:, :, 1], phase)
    turned = jnp.stack([turned_real, turned_imag], axis=2)
    return jnp.where(upper_half, turned, summed)


def ascend(own_field, far_field, self_index, level_bit):
    half_span = 1 << level_bit
    full_span = 2 * half_span
    within = self_index % full_span
    upper_half = within >= half_span
    phase = 2.0 * math.pi / full_span * (within % half_span).astype(jnp.float32)
    own_real, own_imag = rotate(own_field[:, :, 0], own_field[:, :, 1], phase)
    far_real, far_imag = rotate(far_field[:, :, 0], far_field[:, :, 1], phase)
    lower_value = own_field + jnp.stack([far_real, far_imag], axis=2)
    upper_value = far_field - jnp.stack([own_real, own_imag], axis=2)
    return jnp.where(upper_half, upper_value, lower_value)


def forward_levels(samples):
    axis_size = lax.axis_size("ctx")
    self_index = lax.axis_index("ctx")
    tokens = samples.shape[-1]
    length = tokens * axis_size
    top_bit = axis_size.bit_length() - 2
    series = jnp.arange(tokens, dtype=jnp.int32)
    received = partner_2(samples, "ctx", top_bit)
    partner = self_index ^ 1 << top_bit
    own_field = signals(samples, self_index * tokens + series, length)
    far_field = signals(received, partner * tokens + series, length)
    current = descend(own_field, far_field, self_index, top_bit)
    for level_bit in range(top_bit - 1, -1, -1):
        current = descend(current, partner_2(current, "ctx", level_bit), self_index, level_bit)
    return current


def inverse_levels(current):
    axis_size = lax.axis_size("ctx")
    self_index = lax.axis_index("ctx")
    for level_bit in range(axis_size.bit_length() - 1):
        current = ascend(current, partner_2(current, "ctx", level_bit), self_index, level_bit)
    return current


def per_device(output_gradient, input_spectrum, filter_spectrum):
    axis_size = lax.axis_size("ctx")
    self_index = lax.axis_index("ctx")
    tokens = output_gradient.shape[-1]
    length = tokens * axis_size
    sections = axis_size.bit_length() - 1
    current = forward_levels(output_gradient)
    series = jnp.arange(tokens, dtype=jnp.int32)
    residue = reverse(self_index, sections)
    phase = -2.0 * math.pi / length * (residue * series).astype(jnp.float32)
    grad_real, grad_imag = rotate(current[:, :, 0], current[:, :, 1], phase)
    grad_real, grad_imag = local_dft(grad_real, grad_imag, -1.0)
    saved_real = input_spectrum[:, :, 0]
    saved_imag = input_spectrum[:, :, 1]
    term_real = jnp.sum(grad_real * saved_real + grad_imag * saved_imag, axis=0)
    term_imag = jnp.sum(grad_imag * saved_real - grad_real * saved_imag, axis=0)
    filter_gradient = lax.psum_scatter(
        jnp.stack([term_real, term_imag], axis=1), "dp", scatter_dimension=2, tiled=True
    )
    filter_real = filter_spectrum[:, 0]
    filter_imag = filter_spectrum[:, 1]
    prod_real = grad_real * filter_real + grad_imag * filter_imag
    prod_imag = grad_imag * filter_real - grad_real * filter_imag
    prod_real, prod_imag = local_dft(prod_real, prod_imag, 1.0)
    prod_real, prod_imag = rotate(prod_real, prod_imag, -phase)
    current = jnp.stack([prod_real, prod_imag], axis=2)
    current = inverse_levels(current)
    positions = self_index * tokens + series
    phase_back = 0.5 * math.pi / length * positions.astype(jnp.float32)
    turned = current[:, :, 0] * jnp.cos(phase_back) - current[:, :, 1] * jnp.sin(phase_back)
    input_gradient = turned / length
    return (input_gradient, filter_gradient)


def solution(mesh):
    in_specs = (P("dp", None, "ctx"), P("dp", None, None, "ctx"), P(None, None, "ctx"))
    out_specs = (P("dp", None, "ctx"), P(None, None, ("ctx", "dp")))
    return jax.shard_map(
        per_device, mesh=mesh, in_specs=in_specs, out_specs=out_specs, check_vma=False
    )
```

profile of v0, /device:TPU:0, one launch (start us, length us, event | category | flops | bytes accessed | tf_op | source)
XLA Modules:
  0.0 160.4 jit_solution(9251760703301586143)
XLA Ops:
  7.2 4.1 %collective-permute-start = (f32[1,8,8192]{2,1,0:T(8,128)}, f32[1,8,8192]{2,1,0:T(8,128)S(1)}, u32[]{:S(2)}, u32[]{:S(2)}) collective-permute-start(f32[1,8,8192]{2,1,0:T(8,128)} %param.3), channel_id=1, source_target_pairs={{0,2},{1,3},{2,0},{3,1},{4,6},{5,7},{6,4},{7,5},{8,10},{9,11},{10,... | collective-permute-start | bytes 786440 | tf_op jit(solution)/shard_map/ppermute | solution.py:14
  11.8 0.1 fusion.72
  12.0 1.0 multiply_bitcast_fusion.1
  13.0 2.6 %slice_reduce_fusion.1 = (f32[8,8192]{1,0:T(8,128)S(1)}, f32[8,8192]{1,0:T(8,128)S(1)}) fusion(f32[8,2,8192]{2,1,0:T(2,128)} %param.5), kind=kLoop, calls=%fused_computation.58 | loop fusion | bytes 1048576 | tf_op jit(solution)/shard_map/slice | solution.py:146
  15.6 0.2 broadcast_in_dim_squeeze.8
  15.8 0.2 broadcast_in_dim_squeeze.9
  16.0 0.1 fusion.76
  16.2 7.3 %collective-permute-done = f32[1,8,8192]{2,1,0:T(8,128)S(1)} collective-permute-done((f32[1,8,8192]{2,1,0:T(8,128)}, f32[1,8,8192]{2,1,0:T(8,128)S(1)}, u32[]{:S(2)}, u32[]{:S(2)}) %collective-permute-start) | collective-permute-done | bytes 262176 | tf_op jit(solution)/shard_map/ppermute | solution.py:14
  23.7 0.9 collective-permute-start.1
  24.6 0.1 fusion.74
  24.7 0.1 fusion.58
  24.9 0.1 fusion.56
  25.0 0.1 fusion.48
  25.2 0.3 fusion.31
  25.4 11.5 %collective-permute-done.1 = f32[1,8,2,8192]{3,1,2,0:T(8,128)S(1)} collective-permute-done((f32[1,8,2,8192]{3,1,2,0:T(8,128)S(1)}, f32[1,8,2,8192]{3,1,2,0:T(8,128)S(1)}, u32[]{:S(2)}, u32[]{:S(2)}) %collective-permute-start.1) | collective-permute-done | bytes 524320 | tf_op jit(solution)/shard_map/ppermute | solution.py:14
  37.2 0.2 squeeze.12
  37.4 0.2 squeeze.13
  37.7 1.1 fusion.16
  38.8 1.1 fusion.15
  39.9 1.1 fusion.4
  41.0 1.1 fusion.5
  42.1 0.5 fusion.35
  42.7 0.5 fusion.34
  43.2 0.6 convolution_add_fusion.2
  43.8 0.5 convolution_subtract_fusion.2
  44.3 0.1 reshape.1276
  44.5 0.1 reshape.1277
  44.7 0.1 multiply_add_fusion
  44.8 1.0 fusion.23
  45.8 1.2 fusion.21
  47.1 1.0 fusion.3
  48.1 1.0 fusion.2
  49.1 0.5 fusion.37
  49.7 0.5 fusion
  50.4 0.6 fusion.36
  50.9 0.5 fusion.1
  51.8 1.6 %collective-permute-start.2 = (f32[1,8,2,8192]{3,1,2,0:T(8,128)S(1)}, f32[1,8,2,8192]{3,1,2,0:T(8,128)S(1)}, u32[]{:S(2)}, u32[]{:S(2)}) collective-permute-start(f32[1,8,2,8192]{3,1,2,0:T(8,128)S(1)} %pad_maximum_fusion.2), channel_id=1, source_target_pairs={{0,1},{1,0},{2,3},{3,2},{4,5},{5,4},{6,7},{7,6},{8,9},{9,8},{10,11... | collective-permute-start | bytes 1572872 | tf_op jit(solution)/shard_map/ppermute | solution.py:14
  53.4 0.6 fusion.13
  54.0 0.5 pad_maximum_fusion.3
  54.5 16.1 %copy.53 = f32[8,2,8192]{1,0,2:T(8,128)} copy(f32[8,2,8192]{2,1,0:T(2,128)S(1)} %pad_maximum_fusion.3) | data formatting | bytes 1048576
  70.6 21.4 %reshape.1292 = f32[8192,16]{1,0:T(8,128)} reshape(f32[8192,8,2]{2,1,0:T(8,128)} %bitcast.114) | data formatting | bytes 1048576
  92.2 3.3 %collective-permute-start.3 = (f32[1,8,2,8192]{3,1,2,0:T(8,128)S(1)}, f32[1,8,2,8192]{3,1,2,0:T(8,128)S(1)}, u32[]{:S(2)}, u32[]{:S(2)}) collective-permute-start(f32[1,8,2,8192]{3,1,2,0:T(8,128)S(1)} %fusion.6), channel_id=1, source_target_pairs={{0,2},{1,3},{2,0},{3,1},{4,6},{5,7},{6,4},{7,5},{8,10},{9,11},{10,... | collective-permute-start | bytes 1572872 | tf_op jit(solution)/shard_map/ppermute | solution.py:14
  95.5 0.8 multiply_subtract_fusion.3
  96.3 48.1 %reduce-scatter.4.cloned.1.call-done = f32[1024,16]{1,0:T(8,128)} async-done(((f32[8192,16]{1,0:T(8,128)}), f32[1024,16]{1,0:T(8,128)}) %reduce-scatter.4.cloned.1.call-update) | async-done | bytes 65552
  144.4 3.7 %reshape.1293 = f32[1024,8,2]{2,1,0:T(8,128)} reshape(f32[1024,16]{1,0:T(8,128)} %reduce-scatter.4.cloned.1.call-done) | data formatting | bytes 131072
  148.1 3.5 %copy.54 = f32[8,2,1024]{2,1,0:T(2,128)} copy(f32[8,2,1024]{1,0,2:T(8,128)} %bitcast.115) | data formatting | bytes 131072
  151.6 1.1 fusion.7
  152.8 0.8 fusion.11
  (25 shorter events, 1.2 us)
Async XLA Ops:
  7.2 137.2 %reduce-scatter.4.cloned.1.call-start = ((), (), s32[]{:S(2)}) async-start(), calls=%async_computation.1 | async-start | bytes 4718592
  7.2 16.2 %collective-permute-start = (f32[1,8,8192]{2,1,0:T(8,128)}, f32[1,8,8192]{2,1,0:T(8,128)S(1)}, u32[]{:S(2)}, u32[]{:S(2)}) collective-permute-start(f32[1,8,8192]{2,1,0:T(8,128)} %param.3), channel_id=1, source_target_pairs={{0,2},{1,3},{2,0},{3,1},{4,6},{5,7},{6,4},{7,5},{8,10},{9,11},{10,... | collective-permute-start | bytes 786440 | tf_op jit(solution)/shard_map/ppermute | solution.py:14
  23.7 13.2 %collective-permute-start.1 = (f32[1,8,2,8192]{3,1,2,0:T(8,128)S(1)}, f32[1,8,2,8192]{3,1,2,0:T(8,128)S(1)}, u32[]{:S(2)}, u32[]{:S(2)}) collective-permute-start(f32[1,8,2,8192]{3,1,2,0:T(8,128)S(1)} %maximum_select_fusion), channel_id=1, source_target_pairs={{0,1},{1,0},{2,3},{3,2},{4,5},{5,4},{6,7},{7,6},{8,9},{9,8},{10,11... | collective-permute-start | bytes 1572872 | tf_op jit(solution)/shard_map/ppermute | solution.py:14
  49.7 3.7 %copy-start = (f32[1,8,2,8192]{3,2,1,0:T(2,128)S(1)}, f32[1,8,2,8192]{3,2,1,0:T(2,128)}, u32[]{:S(2)}) copy-start(f32[1,8,2,8192]{3,2,1,0:T(2,128)} %param.4) | copy-start | bytes 1572868
  51.8 40.3 %collective-permute-start.2 = (f32[1,8,2,8192]{3,1,2,0:T(8,128)S(1)}, f32[1,8,2,8192]{3,1,2,0:T(8,128)S(1)}, u32[]{:S(2)}, u32[]{:S(2)}) collective-permute-start(f32[1,8,2,8192]{3,1,2,0:T(8,128)S(1)} %pad_maximum_fusion.2), channel_id=1, source_target_pairs={{0,1},{1,0},{2,3},{3,2},{4,5},{5,4},{6,7},{7,6},{8,9},{9,8},{10,11... | collective-permute-start | bytes 1572872 | tf_op jit(solution)/shard_map/ppermute | solution.py:14
  92.2 59.3 %collective-permute-start.3 = (f32[1,8,2,8192]{3,1,2,0:T(8,128)S(1)}, f32[1,8,2,8192]{3,1,2,0:T(8,128)S(1)}, u32[]{:S(2)}, u32[]{:S(2)}) collective-permute-start(f32[1,8,2,8192]{3,1,2,0:T(8,128)S(1)} %fusion.6), channel_id=1, source_target_pairs={{0,2},{1,3},{2,0},{3,1},{4,6},{5,7},{6,4},{7,5},{8,10},{9,11},{10,... | collective-permute-start | bytes 1572872 | tf_op jit(solution)/shard_map/ppermute | solution.py:14
Sparse Core Ops, SparseCore 0:
  92.1 52.2 reduce-scatter.3
where the time goes:
time: 161 us; the launch traced here: 160 us
  waiting for transfers between devices  66.8 us (41%)
  local copies, waits for them, and re-layouts  48.7 us (30%)
  between operations  14.9 us (9%)
  matrix products  13.1 us (8%)
  starting transfers between devices  9.99 us (6%)
  other arithmetic  6.88 us (4%)
    unnamed x2, waiting for transfers between devices  48.1 us
    unnamed x6, local copies, waits for them, and re-layouts  44.6 us
    ppermute x4, waiting for transfers between devices, partner_2(): return lax.ppermute(value, axis, pairs)  18.7 us
    ppermute x4, starting transfers between devices, partner_2(): return lax.ppermute(value, axis, pairs)  9.96 us
    dot_general x4, matrix products, complex_product(): jnp.einsum(form, left_real, right_imag, precision=precise)  3.4 us
    dot_general x4, matrix products, complex_product(): jnp.einsum(form, left_imag, right_real, precision=precise)  3.24 us
    dot_general x4, matrix products, complex_product(): jnp.einsum(form, left_real, right_real, precision=precise)  3.22 us
    dot_general x4, matrix products, complex_product(): jnp.einsum(form, left_imag, right_imag, precision=precise)  3.22 us
  transfers between devices with their start and end apart: 5, of which 3 were waited for; matrix products, arithmetic and copies ran while one was open for 32% of the time, Pallas kernels for 0%

commit v1 on v0

v1 whole, which is shorter than its diff:
```python
import functools
import math

import jax
import jax.numpy as jnp
import ml_dtypes
import numpy as np
from jax import lax
from jax.experimental import pallas as pl
from jax.experimental.pallas import tpu as pltpu
from jax.sharding import PartitionSpec as P

MESH = pl.DeviceIdType.MESH
LANES = 128


def low_bit(value):
    return value & -value


def reverse(index, sections):
    result = 0 * index
    for level in range(sections):
        result = result | ((index >> level) & 1) << (sections - 1 - level)
    return result


def halves(table):
    table = np.asarray(table, np.float32)
    high = table.astype(ml_dtypes.bfloat16)
    low = (table - high.astype(np.float32)).astype(ml_dtypes.bfloat16)
    return np.stack([high, low])


def make_tables(n_ctx, tokens):
    rows = tokens // LANES
    length = n_ctx * tokens
    sections = n_ctx.bit_length() - 1
    turn = 2.0 * math.pi
    ta, tb = np.arange(rows), np.arange(LANES)
    small = turn / rows * (ta[:, None] * ta[None, :] % rows)
    wide = turn / rows * (ta[:, None] * tb[None, :] % rows)
    second = np.block([[np.cos(wide), np.sin(wide)], [-np.sin(wide), np.cos(wide)]])
    third = np.block([[np.cos(small), -np.sin(small)], [np.sin(small), np.cos(small)]])
    first_all, last_all, turns_all = [], [], []
    for self_index in range(n_ctx):
        shift = reverse(self_index, sections) + 0.25
        owner = self_index ^ np.arange(n_ctx)
        start = (owner[:, None] * tokens + LANES * ta[None, :]).reshape(-1)
        offset = turn / length * (shift * start % length)
        angle = np.tile(small, (1, n_ctx)) + offset[None, :]
        first_all.append(halves(np.concatenate([np.cos(angle), -np.sin(angle)], axis=0)))
        angle = np.tile(wide, (n_ctx, 1)) + offset[:, None]
        last_all.append(
            halves(np.concatenate([np.cos(angle), -np.sin(angle)], axis=1) / length)
        )
        angle = turn / length * (tb[None, :] * (n_ctx * tb[:, None] + shift) % length)
        turns_all.append(
            np.stack([np.cos(angle), -np.sin(angle), np.cos(angle).T, np.sin(angle).T])
        )
    return (
        np.stack(first_all),
        np.stack(last_all),
        np.stack(turns_all).astype(np.float32),
        halves(second),
        halves(third),
    )


def split(value):
    high = value.astype(jnp.bfloat16)
    return high, (value - high.astype(jnp.float32)).astype(jnp.bfloat16)


def product(table, value, contract):
    high, low = split(value)
    dims = (((1,), (contract,)), ((), ()))
    dot = functools.partial(
        lax.dot_general, dimension_numbers=dims, preferred_element_type=jnp.float32
    )
    return dot(table[0], high) + (dot(table[0], low) + dot(table[1], high))


def kernel(
    sizes,
    x_ref,
    saved_ref,
    filt_ref,
    first_hbm,
    last_hbm,
    turns_hbm,
    second_ref,
    third_ref,
    out_ref,
    grad_ref,
    first_ref,
    last_ref,
    turns_ref,
    xs,
    zs,
    rs,
    terms,
    others,
    table_sem,
    fwd_send,
    fwd_recv,
    inv_send,
    inv_recv,
    dp_send,
    dp_recv,
):
    n_dp, n_ctx, chans, rows, groups = sizes
    per_group = chans // groups
    share = rows // n_dp
    repeats = LANES // rows
    dp = lax.axis_index("dp")
    ctx = lax.axis_index("ctx")
    bits = [1 << level for level in range(n_ctx.bit_length() - 1)]
    peers = [lax.rem(dp + step, n_dp) for step in range(n_dp)]

    tables = [
        pltpu.make_async_copy(source.at[ctx], target, table_sem.at[number])
        for number, (source, target) in enumerate(
            [(first_hbm, first_ref), (last_hbm, last_ref), (turns_hbm, turns_ref)]
        )
    ]
    for copy in tables:
        copy.start()

    barrier = pltpu.get_barrier_semaphore()
    for bit in bits:
        pl.semaphore_signal(barrier, inc=1, device_id=(dp, ctx ^ bit), device_id_type=MESH)
    for peer in peers[1:]:
        pl.semaphore_signal(barrier, inc=1, device_id=(peer, ctx), device_id_type=MESH)

    for chan in range(chans):
        xs[chan // per_group, 0, chan % per_group] = x_ref[pl.ds(chan, rows, stride=chans), :]
    pl.semaphore_wait(barrier, len(bits) + n_dp - 1)

    def forward(group, slot):
        bit = low_bit(slot)
        return pltpu.make_async_remote_copy(
            src_ref=xs.at[group, slot - bit],
            dst_ref=xs.at[group, slot],
            send_sem=fwd_send.at[group, slot],
            recv_sem=fwd_recv.at[group, slot],
            device_id=(dp, ctx ^ bit),
            device_id_type=MESH,
        )

    def inverse(group, slot):
        return pltpu.make_async_remote_copy(
            src_ref=zs.at[group, slot],
            dst_ref=rs.at[group, slot],
            send_sem=inv_send.at[group, slot],
            recv_sem=inv_recv.at[group, slot],
            device_id=(dp, ctx ^ low_bit(slot)),
            device_id_type=MESH,
        )

    def exchange(group, step):
        return pltpu.make_async_remote_copy(
            src_ref=terms.at[group, peers[step]],
            dst_ref=others.at[group, step],
            send_sem=dp_send.at[group, step],
            recv_sem=dp_recv.at[group, step],
            device_id=(peers[step], ctx),
            device_id_type=MESH,
        )

    def pass_on(group):
        for bit in bits[::-1]:
            for slot in range(2 * bit, n_ctx, 2 * bit):
                if low_bit(slot) == 2 * bit:
                    forward(group, slot).wait_recv()
                forward(group, slot + bit).start()

    def gather(group):
        for slot in range(1, n_ctx, 2):
            forward(group, slot).wait_recv()

    def transform(group):
        pair = range(per_group)
        block = jnp.concatenate(
            [xs[group, :, chan].reshape(n_ctx * rows, LANES) for chan in pair], axis=1
        )
        stage = product(first_ref, block, 0)
        turned = []
        for chan in pair:
            lanes = slice(chan * LANES, (chan + 1) * LANES)
            real = jnp.concatenate([stage[:rows, lanes]] * repeats, axis=0)
            imag = jnp.concatenate([stage[rows:, lanes]] * repeats, axis=0)
            cosine, sine = turns_ref[0], turns_ref[1]
            turned.append(
                jnp.concatenate(
                    [real * cosine - imag * sine, real * sine + imag * cosine], axis=1
                )
            )
        spectrum = product(second_ref, jnp.concatenate(turned, axis=0), 1)
        multiplied = []
        for chan in pair:
            lanes = slice(chan * LANES, (chan + 1) * LANES)
            real, imag = spectrum[:rows, lanes], spectrum[rows:, lanes]
            base = (group * per_group + chan) * 2 * rows
            saved_real = saved_ref[pl.ds(base, rows, stride=2), :]
            saved_imag = saved_ref[pl.ds(base + 1, rows, stride=2), :]
            parts = (real * saved_real + imag * saved_imag, imag * saved_real - real * saved_imag)
            for number, part in enumerate(parts):
                for owner in range(n_dp):
                    where = pl.ds(chan * 2 * share + number, share, stride=2)
                    terms[group, owner, where, :] = part[owner * share : (owner + 1) * share]
            filt_real = filt_ref[pl.ds(base, rows, stride=2), :]
            filt_imag = filt_ref[pl.ds(base + 1, rows, stride=2), :]
            multiplied.append(
                jnp.concatenate(
                    [real * filt_real + imag * filt_imag, imag * filt_real - real * filt_imag],
                    axis=0,
                )
            )
        stage = product(third_ref, jnp.concatenate(multiplied, axis=1), 0)
        turned = []
        for chan in pair:
            lanes = slice(chan * LANES, (chan + 1) * LANES)
            real = jnp.concatenate([stage[:rows, lanes]] * repeats, axis=0)
            imag = jnp.concatenate([stage[rows:, lanes]] * repeats, axis=0)
            cosine, sine = turns_ref[2], turns_ref[3]
            turned.append(
                jnp.concatenate(
                    [real * cosine - imag * sine, real * sine + imag * cosine], axis=1
                )
            )
        result = product(last_ref, jnp.concatenate(turned, axis=0), 1)
        for chan in pair:
            lanes = slice(chan * LANES, (chan + 1) * LANES)
            zs[group, :, chan] = result[:, lanes].reshape(n_ctx, rows, LANES)

    def send_back(group):
        for slot in range(1, n_ctx, 2):
            inverse(group, slot).start()

    def fold(group):
        for bit in bits[:-1]:
            for slot in range(2 * bit, n_ctx, 2 * bit):
                inverse(group, slot + bit).wait_recv()
                zs[group, slot] = zs[group, slot] + rs[group, slot + bit]
                if low_bit(slot) == 2 * bit:
                    inverse(group, slot).start()

    def finish(group):
        for bit in bits:
            inverse(group, bit).wait_recv()
        for chan in range(per_group):
            total = zs[group, 0, chan]
            for bit in bits:
                total = total + rs[group, bit, chan]
            out_ref[pl.ds(group * per_group + chan, rows, stride=chans), :] = total

    for group in range(groups):
        for bit in bits[::-1]:
            forward(group, bit).start()
    pass_on(0)
    for copy in tables:
        copy.wait()
    if groups > 1:
        pass_on(1)
    for group in range(groups):
        gather(group)
        transform(group)
        send_back(group)
        for step in range(1, n_dp):
            exchange(group, step).start()
        if group + 2 < groups:
            pass_on(group + 2)
        if group > 0:
            fold(group - 1)
    fold(groups - 1)
    for group in range(groups):
        finish(group)
        total = terms[group, dp]
        for step in range(1, n_dp):
            exchange(group, step).wait_recv()
            total = total + others[group, step]
        grad_ref[group] = total
    for group in range(groups):
        for slot in range(1, n_ctx):
            forward(group, slot).wait_send()
            inverse(group, slot).wait_send()
        for step in range(1, n_dp):
            exchange(group, step).wait_send()


def per_device(n_dp, n_ctx, output_gradient, input_spectrum, filter_spectrum):
    _, chans, tokens = output_gradient.shape
    rows = tokens // LANES
    groups = chans // 2
    per_group = chans // groups
    share = rows // n_dp
    first, last, turns, second, third = make_tables(n_ctx, tokens)

    def spectral(array):
        array = array.reshape(chans, 2, rows, LANES).transpose(0, 2, 1, 3)
        return array.reshape(chans * rows * 2, LANES)

    samples = output_gradient.reshape(chans, rows, LANES).transpose(1, 0, 2)
    samples = samples.reshape(rows * chans, LANES)
    vmem = pl.BlockSpec(memory_space=pltpu.VMEM)
    anywhere = pl.BlockSpec(memory_space=pl.ANY)
    block = (groups, n_ctx, per_group, rows, LANES)
    spread = (groups, n_dp, per_group * share * 2, LANES)
    dma = pltpu.SemaphoreType.DMA
    gradient, filter_gradient = pl.pallas_call(
        functools.partial(kernel, (n_dp, n_ctx, chans, rows, groups)),
        out_shape=(
            jax.ShapeDtypeStruct((rows * chans, LANES), jnp.float32),
            jax.ShapeDtypeStruct((groups, per_group * share * 2, LANES), jnp.float32),
        ),
        in_specs=[vmem] * 3 + [anywhere] * 3 + [vmem] * 2,
        out_specs=(vmem, vmem),
        scratch_shapes=[
            pltpu.VMEM(first.shape[1:], jnp.bfloat16),
            pltpu.VMEM(last.shape[1:], jnp.bfloat16),
            pltpu.VMEM(turns.shape[1:], jnp.float32),
            pltpu.VMEM(block, jnp.float32),
            pltpu.VMEM(block, jnp.float32),
            pltpu.VMEM(block, jnp.float32),
            pltpu.VMEM(spread, jnp.float32),
            pltpu.VMEM(spread, jnp.float32),
            dma((3,)),
            dma((groups, n_ctx)),
            dma((groups, n_ctx)),
            dma((groups, n_ctx)),
            dma((groups, n_ctx)),
            dma((groups, n_dp)),
            dma((groups, n_dp)),
        ],
        compiler_params=pltpu.CompilerParams(
            collective_id=0, has_side_effects=True, vmem_limit_bytes=40 * 1024 * 1024
        ),
    )(
        samples,
        spectral(input_spectrum[0]),
        spectral(filter_spectrum),
        jnp.asarray(first),
        jnp.asarray(last),
        jnp.asarray(turns),
        jnp.asarray(second),
        jnp.asarray(third),
    )
    gradient = gradient.reshape(rows, chans, LANES).transpose(1, 0, 2)
    filter_gradient = filter_gradient.reshape(chans, share, 2, LANES).transpose(0, 2, 1, 3)
    return (
        gradient.reshape(1, chans, tokens),
        filter_gradient.reshape(chans, 2, share * LANES),
    )


def solution(mesh):
    in_specs = (P("dp", None, "ctx"), P("dp", None, None, "ctx"), P(None, None, "ctx"))
    out_specs = (P("dp", None, "ctx"), P(None, None, ("ctx", "dp")))
    return jax.shard_map(
        functools.partial(per_device, mesh.shape["dp"], mesh.shape["ctx"]),
        mesh=mesh,
        in_specs=in_specs,
        out_specs=out_specs,
        check_vma=False,
    )
```

time: 161 us -> 57.5 us (0.36)
  waiting for transfers between devices: 66.8 us -> 0 us
  Pallas kernels: 0 us -> 46.8 us
  local copies, waits for them, and re-layouts: 48.7 us -> 9.59 us
  between operations: 14.9 us -> 0.65 us
  matrix products: 13.1 us -> 0 us
  starting transfers between devices: 9.99 us -> 0 us
  other arithmetic: 6.88 us -> 0 us
    unnamed x2 -> x0, waiting for transfers between devices: 48.1 us -> none
    pallas_call x0 -> x1, Pallas kernels: none -> 46.8 us  [per_device(): pl.pallas_call(functools.partial(kernel, (n_dp, n_ctx, chans, rows, group...]
    unnamed x6 -> x18, local copies, waits for them, and re-layouts: 44.6 us -> 9.59 us
    ppermute x4 -> x0, waiting for transfers between devices: 18.7 us -> none  [partner_2(): return lax.ppermute(value, axis, pairs)]
    dot_general x16 -> x0, matrix products: 13.1 us -> none  [the longest x4 3.4 us: complex_product(): jnp.einsum(form, left_real, right_imag, precision=precise)]
    ppermute x4 -> x0, starting transfers between devices: 9.96 us -> none  [partner_2(): return lax.ppermute(value, axis, pairs)]
    slice x2 -> x0, local copies, waits for them, and re-layouts: 2.66 us -> none  [the longest x1 2.63 us: per_device(): filter_real = filter_spectrum[:, 0]]
  transfers between devices with their start and end apart: 5 -> 0, of which waited for: 3 -> 0; matrix products, arithmetic and copies ran while one was open for 32% -> 0% of each run, Pallas kernels for 0% -> 0%
where the time goes in v1:
time: 57.5 us; the launch traced here: 57 us
  Pallas kernels  46.8 us (81%)
  local copies, waits for them, and re-layouts  9.59 us (17%)
  between operations  0.65 us (1%)
    pallas_call x1, Pallas kernels, per_device(): pl.pallas_call(functools.partial(kernel, (n_dp, n_ctx, chans, rows, group...  46.8 us
    unnamed x18, local copies, waits for them, and re-layouts  9.59 us

profile of v1, /device:TPU:0, one launch (start us, length us, event | category | flops | bytes accessed | tf_op | source)
XLA Modules:
  0.0 57.0 jit_solution(9801485814366013990)
XLA Ops:
  0.6 0.0 copy-start
  0.6 1.2 %copy-done = f32[4,4,128,128]{3,2,1,0:T(8,128)S(1)} copy-done((f32[4,4,128,128]{3,2,1,0:T(8,128)S(1)}, f32[4,4,128,128]{3,2,1,0:T(8,128)}, u32[]{:S(2)}) %copy-start) | copy-done | bytes 1048600
  1.9 0.0 copy-start.1
  1.9 1.2 %copy-done.1 = bf16[4,2,256,256]{3,2,1,0:T(8,128)(2,1)S(1)} copy-done((bf16[4,2,256,256]{3,2,1,0:T(8,128)(2,1)S(1)}, bf16[4,2,256,256]{3,2,1,0:T(8,128)(2,1)}, u32[]{:S(2)}) %copy-start.1) | copy-done | bytes 1048600
  3.1 0.0 copy-start.2
  3.1 1.0 %copy-done.2 = f32[1,8,2,8192]{3,2,1,0:T(2,128)S(1)} copy-done((f32[1,8,2,8192]{3,2,1,0:T(2,128)S(1)}, f32[1,8,2,8192]{3,2,1,0:T(2,128)}, u32[]{:S(2)}) %copy-start.2) | copy-done | bytes 524312
  4.1 0.0 copy-start.3
  4.1 1.0 %copy-done.3 = f32[8,2,8192]{2,1,0:T(2,128)S(1)} copy-done((f32[8,2,8192]{2,1,0:T(2,128)S(1)}, f32[8,2,8192]{2,1,0:T(2,128)}, u32[]{:S(2)}) %copy-start.3) | copy-done | bytes 524312
  5.2 0.0 copy-start.4
  5.2 1.0 %copy-done.4 = bf16[4,2,128,256]{3,2,1,0:T(8,128)(2,1)S(1)} copy-done((bf16[4,2,128,256]{3,2,1,0:T(8,128)(2,1)S(1)}, bf16[4,2,128,256]{3,2,1,0:T(8,128)(2,1)}, u32[]{:S(2)}) %copy-start.4) | copy-done | bytes 524312
  6.2 0.0 copy-start.5
  6.2 0.9 %copy-done.5 = f32[1,8,8192]{2,1,0:T(8,128)S(1)} copy-done((f32[1,8,8192]{2,1,0:T(8,128)S(1)}, f32[1,8,8192]{2,1,0:T(8,128)}, u32[]{:S(2)}) %copy-start.5) | copy-done | bytes 262168
  7.2 0.0 copy-start.6
  7.2 0.9 %copy-done.6 = bf16[2,128,256]{2,1,0:T(8,128)(2,1)S(1)} copy-done((bf16[2,128,256]{2,1,0:T(8,128)(2,1)S(1)}, bf16[2,128,256]{2,1,0:T(8,128)(2,1)}, u32[]{:S(2)}) %copy-start.6) | copy-done | bytes 131096
  8.1 0.0 copy-start.7
  8.1 0.8 %copy-done.7 = bf16[2,128,128]{2,1,0:T(8,128)(2,1)S(1)} copy-done((bf16[2,128,128]{2,1,0:T(8,128)(2,1)S(1)}, bf16[2,128,128]{2,1,0:T(8,128)(2,1)}, u32[]{:S(2)}) %copy-start.7) | copy-done | bytes 65560
  8.9 46.8 %shard_map.95 = (f32[512,128]{1,0:T(8,128)S(1)}, f32[4,32,128]{2,1,0:T(8,128)S(1)}) custom-call(f32[512,128]{1,0:T(8,128)S(1)} %bitcast.27, f32[1024,128]{1,0:T(8,128)S(1)} %bitcast.25, f32[1024,128]{1,0:T(8,128)S(1)} %bitcast.26, bf16[4,2,128,256]{3,2,1,0:T(8,128)(2,1)S(1)} %copy-done.4, bf16[4,2,256,256]{3,2,1,0:T(8,128)(2,1)S(1)} %copy-done.1, ...), custom_call_target="tpu_custom_call" | custom-call | tf_op jit(solution)/shard_map/pallas_call | solution.py:311
  55.7 0.7 %copy.15 = f32[1,8,8192]{2,1,0:T(8,128)} copy(f32[1,8,8192]{2,1,0:T(8,128)S(1)} %bitcast.28) | data formatting | bytes 524288
  56.4 0.6 %copy.16 = f32[8,2,1024]{2,1,0:T(2,128)} copy(f32[8,2,1024]{2,1,0:T(2,128)S(1)} %bitcast.29) | data formatting | bytes 131072
Async XLA Ops:
  0.6 1.2 %copy-start = (f32[4,4,128,128]{3,2,1,0:T(8,128)S(1)}, f32[4,4,128,128]{3,2,1,0:T(8,128)}, u32[]{:S(2)}) copy-start(f32[4,4,128,128]{3,2,1,0:T(8,128)} %constant.12.clone.turns_hbm) | copy-start | bytes 3145732
  1.9 1.2 %copy-start.1 = (bf16[4,2,256,256]{3,2,1,0:T(8,128)(2,1)S(1)}, bf16[4,2,256,256]{3,2,1,0:T(8,128)(2,1)}, u32[]{:S(2)}) copy-start(bf16[4,2,256,256]{3,2,1,0:T(8,128)(2,1)} %constant.11.clone.last_hbm) | copy-start | bytes 3145732
  3.1 1.0 %copy-start.2 = (f32[1,8,2,8192]{3,2,1,0:T(2,128)S(1)}, f32[1,8,2,8192]{3,2,1,0:T(2,128)}, u32[]{:S(2)}) copy-start(f32[1,8,2,8192]{3,2,1,0:T(2,128)} %param.9) | copy-start | bytes 1572868
  4.1 1.0 %copy-start.3 = (f32[8,2,8192]{2,1,0:T(2,128)S(1)}, f32[8,2,8192]{2,1,0:T(2,128)}, u32[]{:S(2)}) copy-start(f32[8,2,8192]{2,1,0:T(2,128)} %param.10) | copy-start | bytes 1572868
  5.2 1.0 %copy-start.4 = (bf16[4,2,128,256]{3,2,1,0:T(8,128)(2,1)S(1)}, bf16[4,2,128,256]{3,2,1,0:T(8,128)(2,1)}, u32[]{:S(2)}) copy-start(bf16[4,2,128,256]{3,2,1,0:T(8,128)(2,1)} %constant.10.clone.first_hbm) | copy-start | bytes 1572868
  6.2 0.9 %copy-start.5 = (f32[1,8,8192]{2,1,0:T(8,128)S(1)}, f32[1,8,8192]{2,1,0:T(8,128)}, u32[]{:S(2)}) copy-start(f32[1,8,8192]{2,1,0:T(8,128)} %param.8) | copy-start | bytes 786436
  7.2 0.9 %copy-start.6 = (bf16[2,128,256]{2,1,0:T(8,128)(2,1)S(1)}, bf16[2,128,256]{2,1,0:T(8,128)(2,1)}, u32[]{:S(2)}) copy-start(bf16[2,128,256]{2,1,0:T(8,128)(2,1)} %constant.13.clone.second_ref) | copy-start | bytes 393220
  8.1 0.8 %copy-start.7 = (bf16[2,128,128]{2,1,0:T(8,128)(2,1)S(1)}, bf16[2,128,128]{2,1,0:T(8,128)(2,1)}, u32[]{:S(2)}) copy-start(bf16[2,128,128]{2,1,0:T(8,128)(2,1)} %constant.14.clone.third_ref) | copy-start | bytes 196612

commit v2 on v1

--- a/solution.py
+++ b/solution.py
@@ -83,19 +83,24 @@
 
 def kernel(
     sizes,
-    x_ref,
-    saved_ref,
-    filt_ref,
+    x_hbm,
+    saved_hbm,
+    filt_hbm,
     first_hbm,
     last_hbm,
     turns_hbm,
-    second_ref,
-    third_ref,
+    second_hbm,
+    third_hbm,
     out_ref,
     grad_ref,
+    x_ref,
     first_ref,
+    turns_ref,
+    second_ref,
+    saved_ref,
+    filt_ref,
+    third_ref,
     last_ref,
-    turns_ref,
     xs,
     zs,
     rs,
@@ -119,9 +124,18 @@
     peers = [lax.rem(dp + step, n_dp) for step in range(n_dp)]
 
     tables = [
-        pltpu.make_async_copy(source.at[ctx], target, table_sem.at[number])
+        pltpu.make_async_copy(source, target, table_sem.at[number])
         for number, (source, target) in enumerate(
-            [(first_hbm, first_ref), (last_hbm, last_ref), (turns_hbm, turns_ref)]
+            [
+                (x_hbm, x_ref),
+                (first_hbm.at[ctx], first_ref),
+                (turns_hbm.at[ctx], turns_ref),
+                (second_hbm, second_ref),
+                (saved_hbm, saved_ref),
+                (filt_hbm, filt_ref),
+                (third_hbm, third_ref),
+                (last_hbm.at[ctx], last_ref),
+            ]
         )
     ]
     for copy in tables:
@@ -133,6 +147,7 @@
     for peer in peers[1:]:
         pl.semaphore_signal(barrier, inc=1, device_id=(peer, ctx), device_id_type=MESH)
 
+    tables[0].wait()
     for chan in range(chans):
         xs[chan // per_group, 0, chan % per_group] = x_ref[pl.ds(chan, rows, stride=chans), :]
     pl.semaphore_wait(barrier, len(bits) + n_dp - 1)
@@ -255,14 +270,21 @@
                 total = total + rs[group, bit, chan]
             out_ref[pl.ds(group * per_group + chan, rows, stride=chans), :] = total
 
-    for group in range(groups):
-        for bit in bits[::-1]:
-            forward(group, bit).start()
+    def spread(group):
+        if group < groups:
+            for bit in bits[::-1]:
+                forward(group, bit).start()
+
+    spread(0)
+    spread(1)
+    for copy in tables[1:]:
+        copy.wait()
     pass_on(0)
-    for copy in tables:
-        copy.wait()
+    spread(2)
     if groups > 1:
         pass_on(1)
+    for group in range(3, groups):
+        spread(group)
     for group in range(groups):
         gather(group)
         transform(group)
@@ -304,7 +326,7 @@
     samples = output_gradient.reshape(chans, rows, LANES).transpose(1, 0, 2)
     samples = samples.reshape(rows * chans, LANES)
     vmem = pl.BlockSpec(memory_space=pltpu.VMEM)
-    anywhere = pl.BlockSpec(memory_space=pl.ANY)
+    far = pl.BlockSpec(memory_space=pltpu.HBM)
     block = (groups, n_ctx, per_group, rows, LANES)
     spread = (groups, n_dp, per_group * share * 2, LANES)
     dma = pltpu.SemaphoreType.DMA
@@ -314,18 +336,23 @@
             jax.ShapeDtypeStruct((rows * chans, LANES), jnp.float32),
             jax.ShapeDtypeStruct((groups, per_group * share * 2, LANES), jnp.float32),
         ),
-        in_specs=[vmem] * 3 + [anywhere] * 3 + [vmem] * 2,
+        in_specs=[far] * 8,
         out_specs=(vmem, vmem),
         scratch_shapes=[
+            pltpu.VMEM((rows * chans, LANES), jnp.float32),
             pltpu.VMEM(first.shape[1:], jnp.bfloat16),
+            pltpu.VMEM(turns.shape[1:], jnp.float32),
+            pltpu.VMEM(second.shape, jnp.bfloat16),
+            pltpu.VMEM((rows * chans * 2, LANES), jnp.float32),
+            pltpu.VMEM((rows * chans * 2, LANES), jnp.float32),
+            pltpu.VMEM(third.shape, jnp.bfloat16),
             pltpu.VMEM(last.shape[1:], jnp.bfloat16),
-            pltpu.VMEM(turns.shape[1:], jnp.float32),
             pltpu.VMEM(block, jnp.float32),
             pltpu.VMEM(block, jnp.float32),
             pltpu.VMEM(block, jnp.float32),
             pltpu.VMEM(spread, jnp.float32),
             pltpu.VMEM(spread, jnp.float32),
-            dma((3,)),
+            dma((8,)),
             dma((groups, n_ctx)),
             dma((groups, n_ctx)),
             dma((groups, n_ctx)),
@@ -334,7 +361,7 @@
             dma((groups, n_dp)),
         ],
         compiler_params=pltpu.CompilerParams(
-            collective_id=0, has_side_effects=True, vmem_limit_bytes=40 * 1024 * 1024
+            collective_id=0, has_side_effects=True, vmem_limit_bytes=63 * 1024 * 1024
         ),
     )(
         samples,

time: 57.5 us -> 48.7 us (0.85)
  local copies, waits for them, and re-layouts: 9.59 us -> 2.33 us
  Pallas kernels: 46.8 us -> 45.5 us
    unnamed x18 -> x4, local copies, waits for them, and re-layouts: 9.59 us -> 2.33 us
    pallas_call x1, Pallas kernels: 46.8 us -> 45.5 us  [per_device(): pl.pallas_call(functools.partial(kernel, (n_dp, n_ctx, chans, rows, group...]
where the time goes in v2:
time: 48.7 us; the launch traced here: 48.5 us
  Pallas kernels  45.5 us (93%)
  local copies, waits for them, and re-layouts  2.33 us (5%)
  between operations  0.65 us (1%)
    pallas_call x1, Pallas kernels, per_device(): pl.pallas_call(functools.partial(kernel, (n_dp, n_ctx, chans, rows, group...  45.5 us
    unnamed x4, local copies, waits for them, and re-layouts  2.33 us

profile of v2, /device:TPU:0, one launch (start us, length us, event | category | flops | bytes accessed | tf_op | source)
XLA Modules:
  0.0 48.5 jit_solution(18191629309047281200)
XLA Ops:
  0.6 45.5 %shard_map.95 = (f32[512,128]{1,0:T(8,128)}, f32[4,32,128]{2,1,0:T(8,128)}) custom-call(f32[512,128]{1,0:T(8,128)} %bitcast.27, f32[1024,128]{1,0:T(8,128)} %bitcast.25, f32[1024,128]{1,0:T(8,128)} %bitcast.26, bf16[4,2,128,256]{3,2,1,0:T(8,128)(2,1)} %constant.10.clone.first_hbm, bf16[4,2,256,256]{3,2,1,0:T(8,128)(2,1)} %constant.11.clone.last_hbm, ...), custom_call_target="tpu_custom_call" | custom-call | tf_op jit(solution)/shard_map/pallas_call | solution.py:333
  46.2 0.0 copy-start
  46.2 1.7 %copy.15 = f32[1,8,8192]{2,1,0:T(8,128)} copy(f32[1,8,8192]{2,1,0:T(8,128)} %bitcast.28) | data formatting | bytes 524288
  47.9 0.0 copy-done
  47.9 0.6 %copy.16 = f32[8,2,1024]{2,1,0:T(2,128)} copy(f32[8,2,1024]{2,1,0:T(2,128)S(1)} %bitcast.29) | data formatting | bytes 131072
Async XLA Ops:
  46.2 1.7 %copy-start = (f32[4,32,128]{2,1,0:T(8,128)S(1)}, f32[4,32,128]{2,1,0:T(8,128)}, u32[]{:S(2)}) copy-start(f32[4,32,128]{2,1,0:T(8,128)} %get-tuple-element.5) | copy-start | bytes 196612

commit v3 on v2

--- a/solution.py
+++ b/solution.py
@@ -12,10 +12,6 @@
 
 MESH = pl.DeviceIdType.MESH
 LANES = 128
-
-
-def low_bit(value):
-    return value & -value
 
 
 def reverse(index, sections):
@@ -45,7 +41,7 @@
     first_all, last_all, turns_all = [], [], []
     for self_index in range(n_ctx):
         shift = reverse(self_index, sections) + 0.25
-        owner = self_index ^ np.arange(n_ctx)
+        owner = np.arange(n_ctx)
         start = (owner[:, None] * tokens + LANES * ta[None, :]).reshape(-1)
         offset = turn / length * (shift * start % length)
         angle = np.tile(small, (1, n_ctx)) + offset[None, :]
@@ -120,7 +116,6 @@
     repeats = LANES // rows
     dp = lax.axis_index("dp")
     ctx = lax.axis_index("ctx")
-    bits = [1 << level for level in range(n_ctx.bit_length() - 1)]
     peers = [lax.rem(dp + step, n_dp) for step in range(n_dp)]
 
     tables = [
@@ -142,36 +137,39 @@
         copy.start()
 
     barrier = pltpu.get_barrier_semaphore()
-    for bit in bits:
-        pl.semaphore_signal(barrier, inc=1, device_id=(dp, ctx ^ bit), device_id_type=MESH)
+    for way in (1, n_ctx - 1):
+        near = (dp, lax.rem(ctx + way, n_ctx))
+        pl.semaphore_signal(barrier, inc=1, device_id=near, device_id_type=MESH)
     for peer in peers[1:]:
         pl.semaphore_signal(barrier, inc=1, device_id=(peer, ctx), device_id_type=MESH)
 
     tables[0].wait()
     for chan in range(chans):
-        xs[chan // per_group, 0, chan % per_group] = x_ref[pl.ds(chan, rows, stride=chans), :]
-    pl.semaphore_wait(barrier, len(bits) + n_dp - 1)
-
-    def forward(group, slot):
-        bit = low_bit(slot)
+        xs[chan // per_group, ctx, chan % per_group] = x_ref[pl.ds(chan, rows, stride=chans), :]
+    pl.semaphore_wait(barrier, 2 + n_dp - 1)
+
+    def forward(group, slot, way):
         return pltpu.make_async_remote_copy(
-            src_ref=xs.at[group, slot - bit],
+            src_ref=xs.at[group, slot],
             dst_ref=xs.at[group, slot],
-            send_sem=fwd_send.at[group, slot],
+            send_sem=fwd_send.at[(way + 1) // 2, group, slot],
             recv_sem=fwd_recv.at[group, slot],
-            device_id=(dp, ctx ^ bit),
+            device_id=(dp, lax.rem(ctx + way + n_ctx, n_ctx)),
             device_id_type=MESH,
         )
 
-    def inverse(group, slot):
+    def inverse(group, slot, way):
         return pltpu.make_async_remote_copy(
             src_ref=zs.at[group, slot],
-            dst_ref=rs.at[group, slot],
+            dst_ref=rs.at[(way + 1) // 2, group, slot],
             send_sem=inv_send.at[group, slot],
-            recv_sem=inv_recv.at[group, slot],
-            device_id=(dp, ctx ^ low_bit(slot)),
+            recv_sem=inv_recv.at[(way + 1) // 2, group, slot],
+            device_id=(dp, lax.rem(ctx + way + n_ctx, n_ctx)),
             device_id_type=MESH,
         )
+
+    def has(way, steps):
+        return ctx + steps < n_ctx if way > 0 else ctx >= steps
 
     def exchange(group, step):
         return pltpu.make_async_remote_copy(
@@ -183,16 +181,25 @@
             device_id_type=MESH,
         )
 
+    def arrive(group, step, on):
+        for way in (1, -1):
+
+            @pl.when(has(-way, step))
+            def _():
+                forward(group, ctx - way * step, way).wait_recv()
+
+            if on:
+
+                @pl.when(has(-way, step) & has(way, 1))
+                def _():
+                    forward(group, ctx - way * step, way).start()
+
     def pass_on(group):
-        for bit in bits[::-1]:
-            for slot in range(2 * bit, n_ctx, 2 * bit):
-                if low_bit(slot) == 2 * bit:
-                    forward(group, slot).wait_recv()
-                forward(group, slot + bit).start()
+        for step in range(1, n_ctx - 1):
+            arrive(group, step, True)
 
     def gather(group):
-        for slot in range(1, n_ctx, 2):
-            forward(group, slot).wait_recv()
+        arrive(group, n_ctx - 1, False)
 
     def transform(group):
         pair = range(per_group)
@@ -250,30 +257,43 @@
             zs[group, :, chan] = result[:, lanes].reshape(n_ctx, rows, LANES)
 
     def send_back(group):
-        for slot in range(1, n_ctx, 2):
-            inverse(group, slot).start()
+        for step in range(n_ctx - 1, 0, -1):
+            for way in (1, -1):
+
+                @pl.when(has(way, step) & jnp.logical_not(has(-way, 1)))
+                def _():
+                    inverse(group, ctx + way * step, way).start()
 
     def fold(group):
-        for bit in bits[:-1]:
-            for slot in range(2 * bit, n_ctx, 2 * bit):
-                inverse(group, slot + bit).wait_recv()
-                zs[group, slot] = zs[group, slot] + rs[group, slot + bit]
-                if low_bit(slot) == 2 * bit:
-                    inverse(group, slot).start()
+        for step in range(n_ctx - 1, 0, -1):
+            for way in (1, -1):
+                slot = ctx + way * step
+
+                @pl.when(has(way, step) & has(-way, 1))
+                def _():
+                    inverse(group, slot, way).wait_recv()
+                    zs[group, slot] = zs[group, slot] + rs[(way + 1) // 2, group, slot]
+                    inverse(group, slot, way).start()
 
     def finish(group):
-        for bit in bits:
-            inverse(group, bit).wait_recv()
+        for way in (1, -1):
+
+            @pl.when(has(-way, 1))
+            def _():
+                inverse(group, ctx, way).wait_recv()
+                zs[group, ctx] = zs[group, ctx] + rs[(way + 1) // 2, group, ctx]
+
         for chan in range(per_group):
-            total = zs[group, 0, chan]
-            for bit in bits:
-                total = total + rs[group, bit, chan]
-            out_ref[pl.ds(group * per_group + chan, rows, stride=chans), :] = total
+            where = pl.ds(group * per_group + chan, rows, stride=chans)
+            out_ref[where, :] = zs[group, ctx, chan]
 
     def spread(group):
         if group < groups:
-            for bit in bits[::-1]:
-                forward(group, bit).start()
+            for way in (1, -1):
+
+                @pl.when(has(way, 1))
+                def _():
+                    forward(group, ctx, way).start()
 
     spread(0)
     spread(1)
@@ -304,9 +324,19 @@
             total = total + others[group, step]
         grad_ref[group] = total
     for group in range(groups):
-        for slot in range(1, n_ctx):
-            forward(group, slot).wait_send()
-            inverse(group, slot).wait_send()
+        for way in (1, -1):
+            for step in range(n_ctx - 1):
+
+                @pl.when(has(-way, step) & has(way, 1))
+                def _():
+                    forward(group, ctx - way * step, way).wait_send()
+
+            for step in range(1, n_ctx):
+
+                @pl.when(has(way, step))
+                def _():
+                    inverse(group, ctx + way * step, way).wait_send()
+
         for step in range(1, n_dp):
             exchange(group, step).wait_send()
 
@@ -349,14 +379,14 @@
             pltpu.VMEM(last.shape[1:], jnp.bfloat16),
             pltpu.VMEM(block, jnp.float32),
             pltpu.VMEM(block, jnp.float32),
-            pltpu.VMEM(block, jnp.float32),
+            pltpu.VMEM((2,) + block, jnp.float32),
             pltpu.VMEM(spread, jnp.float32),
             pltpu.VMEM(spread, jnp.float32),
             dma((8,)),
+            dma((2, groups, n_ctx)),
             dma((groups, n_ctx)),
             dma((groups, n_ctx)),
-            dma((groups, n_ctx)),
-            dma((groups, n_ctx)),
+            dma((2, groups, n_ctx)),
             dma((groups, n_dp)),
             dma((groups, n_dp)),
         ],

time: 48.7 us -> 51.5 us (1.057)
  Pallas kernels: 45.5 us -> 48.4 us
    pallas_call x1, Pallas kernels: 45.5 us -> 48.4 us  [per_device(): pl.pallas_call(functools.partial(kernel, (n_dp, n_ctx, chans, rows, group...]
where the time goes in v3:
time: 51.5 us; the launch traced here: 51.3 us
  Pallas kernels  48.4 us (94%)
  local copies, waits for them, and re-layouts  2.33 us (5%)
  between operations  0.65 us (1%)
    pallas_call x1, Pallas kernels, per_device(): pl.pallas_call(functools.partial(kernel, (n_dp, n_ctx, chans, rows, group...  48.4 us
    unnamed x4, local copies, waits for them, and re-layouts  2.33 us

profile of v3, /device:TPU:0, one launch (start us, length us, event | category | flops | bytes accessed | tf_op | source)
XLA Modules:
  0.0 51.3 jit_solution(17426436747938448622)
XLA Ops:
  0.6 48.4 %shard_map.95 = (f32[512,128]{1,0:T(8,128)}, f32[4,32,128]{2,1,0:T(8,128)}) custom-call(f32[512,128]{1,0:T(8,128)} %bitcast.27, f32[1024,128]{1,0:T(8,128)} %bitcast.25, f32[1024,128]{1,0:T(8,128)} %bitcast.26, bf16[4,2,128,256]{3,2,1,0:T(8,128)(2,1)} %constant.10.clone.first_hbm, bf16[4,2,256,256]{3,2,1,0:T(8,128)(2,1)} %constant.11.clone.last_hbm, ...), custom_call_target="tpu_custom_call" | custom-call | tf_op jit(solution)/shard_map/pallas_call | solution.py:363
  49.0 0.0 copy-start
  49.0 1.7 %copy.15 = f32[1,8,8192]{2,1,0:T(8,128)} copy(f32[1,8,8192]{2,1,0:T(8,128)} %bitcast.28) | data formatting | bytes 524288
  50.7 0.0 copy-done
  50.7 0.6 %copy.16 = f32[8,2,1024]{2,1,0:T(2,128)} copy(f32[8,2,1024]{2,1,0:T(2,128)S(1)} %bitcast.29) | data formatting | bytes 131072
Async XLA Ops:
  49.0 1.7 %copy-start = (f32[4,32,128]{2,1,0:T(8,128)S(1)}, f32[4,32,128]{2,1,0:T(8,128)}, u32[]{:S(2)}) copy-start(f32[4,32,128]{2,1,0:T(8,128)} %get-tuple-element.5) | copy-start | bytes 196612

commit v4 on v2

--- a/solution.py
+++ b/solution.py
@@ -314,7 +314,7 @@
 def per_device(n_dp, n_ctx, output_gradient, input_spectrum, filter_spectrum):
     _, chans, tokens = output_gradient.shape
     rows = tokens // LANES
-    groups = chans // 2
+    groups = chans // 4
     per_group = chans // groups
     share = rows // n_dp
     first, last, turns, second, third = make_tables(n_ctx, tokens)
@@ -361,7 +361,7 @@
             dma((groups, n_dp)),
         ],
         compiler_params=pltpu.CompilerParams(
-            collective_id=0, has_side_effects=True, vmem_limit_bytes=63 * 1024 * 1024
+            collective_id=0, has_side_effects=True, vmem_limit_bytes=56 * 1024 * 1024
         ),
     )(
         samples,

time: 48.7 us -> 48.1 us (0.988)
  Pallas kernels: 45.5 us -> 45 us
    pallas_call x1, Pallas kernels: 45.5 us -> 45 us  [per_device(): pl.pallas_call(functools.partial(kernel, (n_dp, n_ctx, chans, rows, group...]
where the time goes in v4:
time: 48.1 us; the launch traced here: 48 us
  Pallas kernels  45 us (94%)
  local copies, waits for them, and re-layouts  2.33 us (5%)
  between operations  0.65 us (1%)
    pallas_call x1, Pallas kernels, per_device(): pl.pallas_call(functools.partial(kernel, (n_dp, n_ctx, chans, rows, group...  45 us
    unnamed x4, local copies, waits for them, and re-layouts  2.33 us

profile of v4, /device:TPU:0, one launch (start us, length us, event | category | flops | bytes accessed | tf_op | source)
XLA Modules:
  0.0 48.0 jit_solution(2082685193543079807)
XLA Ops:
  0.6 45.0 %shard_map.95 = (f32[512,128]{1,0:T(8,128)}, f32[2,64,128]{2,1,0:T(8,128)}) custom-call(f32[512,128]{1,0:T(8,128)} %bitcast.27, f32[1024,128]{1,0:T(8,128)} %bitcast.25, f32[1024,128]{1,0:T(8,128)} %bitcast.26, bf16[4,2,128,256]{3,2,1,0:T(8,128)(2,1)} %constant.10.clone.first_hbm, bf16[4,2,256,256]{3,2,1,0:T(8,128)(2,1)} %constant.11.clone.last_hbm, ...), custom_call_target="tpu_custom_call" | custom-call | tf_op jit(solution)/shard_map/pallas_call | solution.py:333
  45.6 0.0 copy-start
  45.6 1.7 %copy.15 = f32[1,8,8192]{2,1,0:T(8,128)} copy(f32[1,8,8192]{2,1,0:T(8,128)} %bitcast.28) | data formatting | bytes 524288
  47.3 0.0 copy-done
  47.3 0.6 %copy.16 = f32[8,2,1024]{2,1,0:T(2,128)} copy(f32[8,2,1024]{2,1,0:T(2,128)S(1)} %bitcast.29) | data formatting | bytes 131072
Async XLA Ops:
  45.6 1.7 %copy-start = (f32[2,64,128]{2,1,0:T(8,128)S(1)}, f32[2,64,128]{2,1,0:T(8,128)}, u32[]{:S(2)}) copy-start(f32[2,64,128]{2,1,0:T(8,128)} %get-tuple-element.5) | copy-start | bytes 196612
